TPU v7x, 32 devices: a whole 2x2x4 slice. The times are simulated.
32 devices in a mesh: rows: 8 (over z, y), grp: 4 (over x, core).
Axes of the slice: x: 2, y: 2, z: 4, core: 2. Of those that a mesh axis runs over, the one named last changes fastest.
Arguments:
- features: bfloat16 [192, 128, 2048], P('rows', None, 'grp'), may hold values from 0 to 12
- depth_weight: float32 [3, 3, 3, 2048], P(None, None, None, 'grp'), may hold values from -2 to 2
- branch_weight: bfloat16 [4, 2048, 256], P(None, 'grp'), may hold values from -0.125 to 0.125
- pool_weight: bfloat16 [2048, 256], P('grp'), may hold values from -0.125 to 0.125
- proj_weight: bfloat16 [5, 256, 256], P(None, 'grp'), may hold values from -0.15625 to 0.15625
- class_weight: bfloat16 [256, 11], replicated, may hold values from -0.375 to 0.375
- labels: int32 [192, 128], P('rows'), may hold values from 0 to 11
Outputs:
- grad_branch: float32 [4, 2048, 256], P(None, 'grp')
- grad_depth: float32 [3, 3, 3, 2048], P(None, None, None, 'grp')
- grad_pool: float32 [2048, 256], P('grp')
- grad_proj: float32 [5, 256, 256], P(None, 'grp')
- grad_class: float32 [256, 11], replicated
All inputs are finite; a program needn't handle non-finite values.
Results may differ from a plain program's by a relative error of at most 0.0056.
Values may be sent and summed in bfloat16 or wider, within the bound.
A program may use at most 128 MiB of HBM per device.

v0:
```python
import math
import jax
import jax.numpy as jnp
from jax import lax
from jax.sharding import PartitionSpec as P

RATES = (6, 12, 18)
MARGIN = 18


def padded_2(block, sides, width):
    for axis, dim in sides:
        count = lax.axis_size(axis)
        forward = [(i, i + 1) for i in range(count - 1)]
        backward = [(target, source) for source, target in forward]
        low = lax.ppermute(
            lax.slice_in_dim(block, block.shape[dim] - width, None, axis=dim), axis, forward
        )
        high = lax.ppermute(lax.slice_in_dim(block, 0, width, axis=dim), axis, backward)
        block = jnp.concatenate([low, block, high], axis=dim)
    return block


def depth_taps(padded, weights, height, width):
    outputs = []
    for index, rate in enumerate(RATES):
        total = jnp.zeros((height, width, padded.shape[2]), jnp.float32)
        for row_tap in range(3):
            for col_tap in range(3):
                row_start = MARGIN + (row_tap - 1) * rate
                col_start = MARGIN + (col_tap - 1) * rate
                total = (
                    total
                    + weights[index, row_tap, col_tap]
                    * padded[row_start : row_start + height, col_start : col_start + width]
                )
        outputs.append(total.astype(jnp.bfloat16))
    return outputs


def depth_grads(padded, backs, height, width):
    result = []
    for index, rate in enumerate(RATES):
        taps = []
        for row_tap in range(3):
            for col_tap in range(3):
                row_start = MARGIN + (row_tap - 1) * rate
                col_start = MARGIN + (col_tap - 1) * rate
                window = padded[row_start : row_start + height, col_start : col_start + width]
                taps.append(jnp.sum(backs[index] * window, axis=(0, 1)))
        result.append(jnp.stack(taps).reshape(3, 3, -1))
    return jnp.stack(result)


def class_head(mixed, class_weight, labels, total_pixels):
    f32 = jnp.float32
    classes = class_weight.shape[1]
    hidden = jnp.maximum(mixed, 0.0).astype(jnp.bfloat16)
    logits = jnp.einsum("pc,ck->kp", hidden, class_weight, preferred_element_type=f32)
    expo = jnp.exp(logits)
    soft = expo / jnp.sum(expo, axis=0, keepdims=True)
    label_row = labels.reshape(-1)
    onehot = (
        lax.broadcasted_iota(jnp.int32, (classes, label_row.shape[0]), 0) == label_row[None, :]
    ).astype(f32)
    valid = (label_row < classes).astype(f32)
    grad_logit = ((soft - onehot) * valid[None, :] / math.sqrt(total_pixels)).astype(jnp.bfloat16)
    class_part = jnp.einsum("pc,kp->ck", hidden, grad_logit, preferred_element_type=f32)
    back_hidden = jnp.einsum("ck,kp->pc", class_weight, grad_logit, preferred_element_type=f32)
    grad_mixed = (back_hidden * (mixed > 0)).astype(jnp.bfloat16)
    col_total = lax.psum(jnp.sum(grad_mixed.astype(f32), axis=0), "rows")
    return (grad_mixed, col_total, class_part)


def per_device(
    features, depth_weight, branch_weight, pool_weight, proj_weight, class_weight, labels
):
    f32 = jnp.float32
    highest = lax.Precision.HIGHEST
    height, width, local_in = features.shape
    pixels_local = height * width
    total_pixels = height * lax.axis_size("rows") * width
    halo_rows = padded_2(features, (("rows", 0),), MARGIN)
    padded = jnp.pad(halo_rows.astype(f32), ((0, 0), (MARGIN, MARGIN), (0, 0)))
    depth_out = depth_taps(padded, depth_weight, height, width)
    flat_inputs = [item.reshape(pixels_local, local_in) for item in [features] + depth_out]
    column_sum = jnp.sum(features.astype(f32), axis=(0, 1))
    pooled = lax.psum(column_sum, "rows") / total_pixels
    partial_pre = jnp.stack(
        [jnp.dot(flat_inputs[k], branch_weight[k], preferred_element_type=f32) for k in range(4)]
    )
    pool_part = jnp.dot(pooled, pool_weight.astype(f32), precision=highest)[None, None, :]
    pre, pool_pre = (
        lax.psum_scatter(partial_pre, "grp", scatter_dimension=2, tiled=True),
        lax.psum_scatter(pool_part, "grp", scatter_dimension=2, tiled=True),
    )
    pool_pre = pool_pre[0, 0]
    own_out = jnp.maximum(pre, 0.0).astype(jnp.bfloat16)
    own_pool = jnp.maximum(pool_pre, 0.0).astype(jnp.bfloat16)
    mixed_part = jnp.einsum("kpc,kcd->pd", own_out, proj_weight[:4], preferred_element_type=f32)
    mixed_part = (
        mixed_part
        + jnp.dot(own_pool.astype(f32), proj_weight[4].astype(f32), precision=highest)[None, :]
    )
    mixed = lax.psum(mixed_part, "grp")
    grad_mixed, col_total, class_part = class_head(mixed, class_weight, labels, total_pixels)
    back_pre = jnp.einsum("pd,kcd->kpc", grad_mixed, proj_weight[:4], preferred_element_type=f32)
    own_grad = (back_pre * (pre > 0)).astype(jnp.bfloat16)
    own_poolgrad = (
        jnp.dot(col_total, proj_weight[4].astype(f32).T, precision=highest) * (pool_pre > 0)
    ).astype(jnp.bfloat16)
    grad_pre, grad_poolpre = (
        lax.all_gather(own_grad, "grp", axis=2, tiled=True),
        lax.all_gather(own_poolgrad[None, None, :], "grp", axis=2, tiled=True),
    )
    grad_poolpre = grad_poolpre[0, 0]
    proj_part = jnp.einsum("kpc,pd->kcd", own_out, grad_mixed, preferred_element_type=f32)
    pool_proj = own_pool.astype(f32)[:, None] * col_total[None, :]
    branch_part = jnp.stack(
        [
            jnp.einsum("pc,pd->cd", flat_inputs[k], grad_pre[k], preferred_element_type=f32)
            for k in range(4)
        ]
    )
    backs = [
        jnp.einsum(
            "pd,cd->pc", grad_pre[k + 1], branch_weight[k + 1], preferred_element_type=f32
        ).reshape(height, width, local_in)
        for k in range(3)
    ]
    depth_part = depth_grads(padded, backs, height, width)
    grad_pool = pooled[:, None] * grad_poolpre.astype(f32)[None, :]
    grad_branch, grad_depth, proj_main, grad_class = lax.psum(
        (branch_part, depth_part, proj_part, class_part), "rows"
    )
    grad_proj = jnp.concatenate([proj_main, pool_proj[None]], axis=0)
    return (grad_branch, grad_depth, grad_pool, grad_proj, grad_class)


def solution(mesh):
    return jax.shard_map(
        per_device,
        mesh=mesh,
        in_specs=(
            P("rows", None, "grp"),
            P(None, None, None, "grp"),
            P(None, "grp", None),
            P("grp", None),
            P(None, "grp", None),
            P(),
            P("rows", None),
        ),
        out_specs=(
            P(None, "grp", None),
            P(None, None, None, "grp"),
            P("grp", None),
            P(None, "grp", None),
            P(),
        ),
        check_vma=False,
    )
```

profile of v0, /device:TPU:0, one launch (start us, length us, event | category | flops | bytes accessed | tf_op | source)
XLA Modules:
  0.0 927.9 jit_solution(12588569372178841400)
XLA Ops:
  7.2 5.2 fusion.69
  12.4 6.3 collective-permute-start
  18.7 1.3 collective-permute-start.1
  20.4 110.5 %psum.49 = f32[512]{0:T(512)S(1)} all-reduce(f32[512]{0:T(512)S(1)} %convert_reduce_fusion), channel_id=1, replica_groups=mesh['rows'=8,'grp'=4] {'rows'}, use_global_device_ids=true, to_apply=%region_2.3 | all-reduce | flops 512 | bytes 4096 | tf_op jit(solution)/shard_map/psum | solution.py:88
  132.2 1.9 convolution_bitcast_fusion.5
  134.2 8.1 maximum_convert_fusion
  142.3 24.1 %add_convert_fusion.1 = bf16[24,128,512]{2,1,0:T(8,128)(2,1)S(1)} fusion(f32[60,128,512]{2,1,0:T(8,128)} %maximum_convert_fusion, f32[512]{0:T(512)S(1)} %bitcast.242, f32[512]{0:T(512)S(1)} %bitcast.243, f32[512]{0:T(512)S(1)} %bitcast.244, f32[512]{0:T(512)S(1)} %bitcast.245, f32[512]{0:T(512)S(1)} %bitcast.246, f32[512]{0:T(512)S(1)} %bitcast.247, ...), kind=kLoop, calls=%fused_computation.49 | loop fusion | flops 28311552 | bytes 37767168 | tf_op jit(solution)/shard_map/convert_element_type | solution.py:37
  166.3 2.1 convolution_bitcast_fusion.3
  168.5 19.2 %add_convert_fusion = bf16[24,128,512]{2,1,0:T(8,128)(2,1)S(1)} fusion(f32[60,128,512]{2,1,0:T(8,128)} %maximum_convert_fusion, f32[512]{0:T(512)S(1)} %bitcast.230, f32[512]{0:T(512)S(1)} %bitcast.231, f32[512]{0:T(512)S(1)} %bitcast.235, f32[512]{0:T(512)S(1)} %bitcast.236, f32[512]{0:T(512)S(1)} %bitcast.237, f32[512]{0:T(512)S(1)} %bitcast.238, ...), kind=kLoop, calls=%fused_computation.48 | loop fusion | flops 28311552 | bytes 37767168 | tf_op jit(solution)/shard_map/convert_element_type | solution.py:37
  187.7 1.7 copy-done.3
  189.4 3.6 convolution_bitcast_fusion.2
  193.0 24.6 %add_convert_fusion.2 = bf16[24,128,512]{2,1,0:T(8,128)(2,1)S(1)} fusion(f32[60,128,512]{2,1,0:T(8,128)} %maximum_convert_fusion, f32[512]{0:T(512)S(1)} %bitcast.233, f32[512]{0:T(512)S(1)} %bitcast.234, f32[512]{0:T(512)S(1)} %bitcast.225, f32[512]{0:T(512)S(1)} %bitcast.226, f32[512]{0:T(512)S(1)} %bitcast.227, f32[512]{0:T(512)S(1)} %bitcast.228, ...), kind=kLoop, calls=%fused_computation.50 | loop fusion | flops 28311552 | bytes 37767168 | tf_op jit(solution)/shard_map/convert_element_type | solution.py:37
  217.6 1.6 copy-done.5
  219.2 2.4 convolution_bitcast_fusion.4
  221.6 4.9 pad_maximum_fusion
  226.5 15.3 %copy.30 = f32[4,3072,256]{1,0,2:T(4,128)} copy(f32[4,3072,256]{2,1,0:T(8,128)} %pad_maximum_fusion) | data formatting | bytes 25165824 | tf_op jit(solution)/shard_map/stack | solution.py:89
  244.8 217.1 %all-reduce.12.cloned.1.call-done = f32[4,3072,256]{1,0,2:T(4,128)} async-done(((f32[4,3072,256]{1,0,2:T(4,128)}), f32[4,3072,256]{1,0,2:T(4,128)}) %all-reduce.12.cloned.1.call-update) | async-done | bytes 12582928
  461.9 2.1 constant_dynamic-slice_fusion
  464.0 1.6 copy-done.7
  465.6 3.8 fusion.1
  469.5 68.7 %all-reduce.10.cloned.1.call-done = f32[3072,256]{1,0:T(8,128)} async-done(((f32[3072,256]{1,0:T(8,128)}), f32[3072,256]{1,0:T(8,128)}) %all-reduce.10.cloned.1.call-update) | async-done | bytes 3145744 | tf_op jit(solution)/shard_map/psum | solution.py:105
  538.2 2.6 fusion.73
  540.8 3.2 convert_reduce_fusion.1
  544.1 3.3 fusion.3
  547.4 2.4 copy.33
  549.8 2.8 fusion.29
  552.7 5.0 fusion.12
  557.7 38.8 %all-gather.3.cloned.1.call-done = bf16[4,3072,256]{1,0,2:T(4,128)(2,1)} async-done(((bf16[4,3072,64]{1,0,2:T(4,128)(2,1)}), bf16[4,3072,256]{1,0,2:T(4,128)(2,1)}) %all-gather.3.cloned.1.call-update) | async-done | bytes 6291472 | tf_op jit(solution)/shard_map/all_gather | solution.py:113
  596.4 18.7 %fusion.68 = (bf16[1,3072,256]{1,0,2:T(2,128)(2,1)}, bf16[1,3072,256]{1,0,2:T(2,128)(2,1)}, bf16[1,3072,256]{1,0,2:T(2,128)(2,1)}, bf16[1,3072,256]{1,0,2:T(2,128)(2,1)}) fusion(bf16[4,3072,256]{1,0,2:T(4,128)(2,1)} %all-gather.3.cloned.1.call-done), kind=kLoop, calls=%fused_computation.133 | loop fusion | bytes 12582912 | tf_op jit(solution)/shard_map/slice | solution.py:121
  615.2 7.3 copy.48
  622.5 4.3 fusion.18
  626.8 24.8 %multiply_reduce_fusion.18 = (f32[512]{0:T(512)S(1)}, f32[512]{0:T(512)S(1)}, f32[512]{0:T(512)S(1)}, f32[512]{0:T(512)S(1)}, f32[512]{0:T(512)S(1)}, /*index=5*...) fusion(f32[60,128,512]{2,1,0:T(8,128)} %maximum_convert_fusion, ...), kind=kOutput, calls=%fused_computation.38 | convolution fusion | flops 833613312 | bytes 36456448 | tf_op jit(solution)/shard_map/pd,cd->pc/dot_general | solution.py:126
  651.6 7.3 copy.49
  658.9 4.3 fusion.21
  663.2 24.1 %multiply_reduce_fusion.9 = (f32[512]{0:T(512)S(1)}, f32[512]{0:T(512)S(1)}, f32[512]{0:T(512)S(1)}, f32[512]{0:T(512)S(1)}, f32[512]{0:T(512)S(1)}, /*index=5*/...) fusion(f32[60,128,512]{2,1,0:T(8,128)} %maximum_convert_fusion, ...), kind=kOutput, calls=%fused_computation.29 | convolution fusion | flops 833613312 | bytes 36456448 | tf_op jit(solution)/shard_map/pd,cd->pc/dot_general | solution.py:126
  687.4 7.3 copy.50
  694.7 4.2 fusion.24
  698.9 20.2 %multiply_reduce_fusion = (f32[512]{0:T(512)S(1)}, f32[512]{0:T(512)S(1)}, f32[512]{0:T(512)S(1)}, f32[512]{0:T(512)S(1)}, f32[512]{0:T(512)S(1)}, /*index=5*/f3...) fusion(f32[60,128,512]{2,1,0:T(8,128)} %maximum_convert_fusion, bf16[24,128,256]{2,1,0:T(8,128)(2,1)} %bitcast.217, ...), kind=kOutput, calls=%fused_computation.20 | convolution fusion | flops 833613312 | bytes 36456448 | tf_op jit(solution)/shard_map/pd,cd->pc/dot_general | solution.py:126
  719.2 7.3 copy.47
  726.5 3.2 fusion.15
  730.5 3.0 pad_maximum_fusion.1
  734.1 66.5 %all-reduce.14.cloned.1.call-done = (f32[3,3,3,512]{3,2,1,0:T(4,128)}, f32[256]{0:T(256)}, f32[256,11]{0,1:T(8,128)}) async-done(((f32[3,3,3,512]{3,2,1,0:T(4,128)}, f32[256]{0:T(256)}, f32[256,11]{0,1:T(8,128)}), (f32[3,3,3,512]{3,2,1,0:T(4,128)}, f32[256]{0:T(256)}, f32[256,11]{0,1:T(8,128)})) %all-reduce.14.cloned.1.call-update) | async-done | bytes 67600 | tf_op jit(solution)/shard_map/psum | solution.py:133
  801.8 5.6 all-reduce.1
  809.1 104.3 %all-reduce.16.cloned.1.call-done = (f32[4,512,256]{1,2,0:T(8,128)}, f32[4,64,256]{2,1,0:T(8,128)}) async-done(((f32[4,512,256]{1,2,0:T(8,128)}, f32[4,64,256]{2,1,0:T(8,128)}), (f32[4,512,256]{1,2,0:T(8,128)}, f32[4,64,256]{2,1,0:T(8,128)})) %all-reduce.16.cloned.1.call-update) | async-done | bytes 2359312 | tf_op jit(solution)/shard_map/psum | solution.py:133
  913.4 2.9 copy.41
  916.3 1.7 pad_maximum_fusion.2
  918.0 1.5 copy.63
  919.5 1.3 copy.64
  (69 shorter events, 7.9 us)
Async XLA Ops:
  7.2 123.8 %copy-start = (bf16[512,256]{1,0:T(8,128)(2,1)S(1)}, bf16[512,256]{1,0:T(8,128)(2,1)}, u32[]{:S(2)}) copy-start(bf16[512,256]{1,0:T(8,128)(2,1)} %param.10) | copy-start | bytes 786436
  7.2 12.8 %copy-start.2 = (bf16[24,128,512]{2,1,0:T(8,128)(2,1)S(1)}, bf16[24,128,512]{2,1,0:T(8,128)(2,1)}, u32[]{:S(2)}) copy-start(bf16[24,128,512]{2,1,0:T(8,128)(2,1)} %param.7) | copy-start | bytes 9437188
  7.2 125.0 %copy-start.13 = (f32[3,3,3,512]{3,2,1,0:T(4,128)S(1)}, f32[3,3,3,512]{3,2,1,0:T(4,128)}, u32[]{:S(2)}) copy-start(f32[3,3,3,512]{3,2,1,0:T(4,128)} %param.8) | copy-start | bytes 165892
  7.2 236.6 %reduce-scatter.4.cloned.1.call-start = ((), (), s32[]{:S(2)}) async-start(), calls=%async_computation.3 | async-start | bytes 163840
  12.4 121.8 %collective-permute-start = (bf16[18,128,512]{2,1,0:T(8,128)(2,1)}, bf16[18,128,512]{2,1,0:T(8,128)(2,1)}, u32[]{:S(2)}, u32[]{:S(2)}) collective-permute-start(bf16[18,128,512]{2,1,0:T(8,128)(2,1)} %get-tuple-element.56), channel_id=1, source_target_pairs={{0,4},{4,8},{8,12},{12,16},{16,20},{20,24},{24,28},{1,5},{5,9},{9,... | collective-permute-start | bytes 7077896 | tf_op jit(solution)/shard_map/ppermute | solution.py:16
  18.7 115.5 %collective-permute-start.1 = (bf16[18,128,512]{2,1,0:T(8,128)(2,1)}, bf16[18,128,512]{2,1,0:T(8,128)(2,1)}, u32[]{:S(2)}, u32[]{:S(2)}) collective-permute-start(bf16[18,128,512]{2,1,0:T(8,128)(2,1)} %get-tuple-element.57), channel_id=1, source_target_pairs={{4,0},{8,4},{12,8},{16,12},{20,16},{24,20},{28,24},{5,1},{9,5},{13... | collective-permute-start | bytes 7077896 | tf_op jit(solution)/shard_map/ppermute | solution.py:19
  132.1 329.7 %all-reduce.12.cloned.1.call-start = ((), (), s32[]{:S(2)}) async-start(), calls=%async_computation.4 | async-start | bytes 25165824
  166.3 2.1 copy-start.4
  187.7 1.7 copy-start.3
  217.6 1.6 copy-start.5
  217.6 4.0 copy-start.6
  241.8 0.7 copy-start.16
  241.8 2.8 copy-start.15
  241.9 296.4 %all-reduce.10.cloned.1.call-start = ((), (), s32[]{:S(2)}) async-start(), calls=%async_computation.1 | async-start | bytes 6291456 | tf_op jit(solution)/shard_map/psum | solution.py:105
  464.0 1.7 copy-start.7
  464.0 5.5 copy-start.12
  464.0 74.3 %copy-start.14 = (bf16[256,11]{0,1:T(8,128)(2,1)S(1)}, bf16[256,11]{0,1:T(8,128)(2,1)}, u32[]{:S(2)}) copy-start(bf16[256,11]{0,1:T(8,128)(2,1)} %param.12) | copy-start | bytes 16900
  469.4 127.0 %all-gather.3.cloned.1.call-start = ((), (), s32[]{:S(2)}) async-start(), calls=%async_computation.2 | async-start | bytes 7864320 | tf_op jit(solution)/shard_map/all_gather | solution.py:113
  538.2 5.8 copy-start.8
  544.1 3.3 copy-start.9
  549.8 250.9 %all-reduce.14.cloned.1.call-start = ((), (), s32[]{:S(2)}) async-start(), calls=%async_computation.5 | async-start | bytes 182272 | tf_op jit(solution)/shard_map/psum | solution.py:133
  622.5 4.3 copy-start.10
  658.9 4.3 copy-start.11
  726.5 194.3 %copy-start.1 = (bf16[512,256]{1,0:T(8,128)(2,1)S(1)}, bf16[512,256]{1,0:T(8,128)(2,1)}, u32[]{:S(2)}) copy-start(bf16[512,256]{1,0:T(8,128)(2,1)} %param.10) | copy-start | bytes 786436
  730.4 183.0 %all-reduce.16.cloned.1.call-start = ((), (), s32[]{:S(2)}) async-start(), calls=%async_computation.6 | async-start | bytes 4718592 | tf_op jit(solution)/shard_map/psum | solution.py:133
Sparse Core Ops, SparseCore 0:
  132.2 18.7 reduce-scatter.3
  242.0 219.8 all-reduce.11
  469.5 68.6 all-reduce.9
  549.9 46.4 all-gather.2
  730.5 70.0 all-reduce.13
  805.1 108.2 all-reduce.15
where the time goes:
time: 932 us; the launch traced here: 928 us
  waiting for transfers between devices  496 us (53%)
  matrix products  118 us (13%)
  blocking collectives  116 us (12%)
  other arithmetic  88.4 us (9%)
  local copies, waits for them, and re-layouts  85.7 us (9%)
  between operations  15.9 us (2%)
    unnamed x8, waiting for transfers between devices  217 us
    psum x2, waiting for transfers between devices, per_device(): lax.psum((branch_part, depth_part, proj_part, class_part), 'rows')  171 us
    psum x1, blocking collectives, per_device(): pooled = lax.psum(column_sum, 'rows') / total_pixels  111 us
    dot_general x3, matrix products, per_device(): jnp.einsum('pd,cd->pc', grad_pre[k + 1], branch_weight[k + 1], preferred_...  69 us
    psum x1, waiting for transfers between devices, per_device(): mixed = lax.psum(mixed_part, 'grp')  68.7 us
    convert_element_type x3, other arithmetic, depth_taps(): outputs.append(total.astype(jnp.bfloat16))  67.9 us
    unnamed x46, local copies, waits for them, and re-layouts  43.9 us
    all_gather x1, waiting for transfers between devices, per_device(): lax.all_gather(own_grad, 'grp', axis=2, tiled=True)  38.8 us
  transfers between devices with their start and end apart: 8, of which 5 were waited for; matrix products, arithmetic and copies ran while one was open for 13% of the time, Pallas kernels for 0%

commit v1 on v0

--- a/solution.py
+++ b/solution.py
@@ -6,6 +6,27 @@
 
 RATES = (6, 12, 18)
 MARGIN = 18
+
+
+def ring_gather(value, axis, dim):
+    size, position, rows = (lax.axis_size(axis), lax.axis_index(axis), value.shape[dim])
+    right = [(i, (i + 1) % size) for i in range(size)]
+    downward = [(i, (i - 1) % size) for i in range(size)]
+    out = jnp.zeros((*value.shape[:dim], size * rows, *value.shape[dim + 1 :]), value.dtype)
+    out = lax.dynamic_update_slice_in_dim(out, value, position * rows, axis=dim)
+    from_left = from_right = value
+    half = size // 2
+    for step in range(1, half + 1):
+        from_left = lax.ppermute(from_left, axis, right)
+        out = lax.dynamic_update_slice_in_dim(
+            out, from_left, (position - step) % size * rows, axis=dim
+        )
+        if step < size - half:
+            from_right = lax.ppermute(from_right, axis, downward)
+            out = lax.dynamic_update_slice_in_dim(
+                out, from_right, (position + step) % size * rows, axis=dim
+            )
+    return out
 
 
 def padded_2(block, sides, width):
@@ -110,7 +131,7 @@
         jnp.dot(col_total, proj_weight[4].astype(f32).T, precision=highest) * (pool_pre > 0)
     ).astype(jnp.bfloat16)
     grad_pre, grad_poolpre = (
-        lax.all_gather(own_grad, "grp", axis=2, tiled=True),
+        ring_gather(own_grad, "grp", 2),
         lax.all_gather(own_poolgrad[None, None, :], "grp", axis=2, tiled=True),
     )
     grad_poolpre = grad_poolpre[0, 0]

time: 932 us -> 1030 us (1.11)
  local copies, waits for them, and re-layouts: 85.7 us -> 186 us
  waiting for transfers between devices: 496 us -> 481 us
  starting transfers between devices: 8.31 us -> 21.5 us
    dynamic_update_slice x0 -> x4, local copies, waits for them, and re-layouts: none -> 128 us  [the longest x2 62.9 us: ring_gather(): lax.dynamic_update_slice_in_dim(out, from_left, (position - step) % size...]
    all_gather x1 -> x0, waiting for transfers between devices: 38.8 us -> none  [per_device(): lax.all_gather(own_grad, 'grp', axis=2, tiled=True)]
    ppermute x0 -> x3, waiting for transfers between devices: none -> 34.6 us  [the longest x2 34.6 us: ring_gather(): from_left = lax.ppermute(from_left, axis, right)]
    unnamed x46 -> x56, local copies, waits for them, and re-layouts: 43.9 us -> 13.6 us
    slice x1, local copies, waits for them, and re-layouts: 18.7 us -> 4.53 us  [per_device(): grad_pre[k]]
    ppermute x0 -> x3, local copies, waits for them, and re-layouts: none -> 12.5 us  [the longest x2 8.31 us: ring_gather(): from_left = lax.ppermute(from_left, axis, right)]
    unnamed x8 -> x7, waiting for transfers between devices: 217 us -> 206 us
    psum x1, starting transfers between devices: 0.57 us -> 12.1 us  [per_device(): mixed = lax.psum(mixed_part, 'grp')]
  transfers between devices with their start and end apart: 8 -> 10, of which waited for: 5 -> 5; matrix products, arithmetic and copies ran while one was open for 13% -> 23% of each run, Pallas kernels for 0% -> 0%
where the time goes in v1:
time: 1030 us; the launch traced here: 1020 us
  waiting for transfers between devices  481 us (47%)
  local copies, waits for them, and re-layouts  186 us (18%)
  blocking collectives  116 us (11%)
  matrix products  114 us (11%)
  other arithmetic  87.9 us (9%)
  starting transfers between devices  21.5 us (2%)
  between operations  15.7 us (2%)
    unnamed x7, waiting for transfers between devices  206 us
    psum x2, waiting for transfers between devices, per_device(): lax.psum((branch_part, depth_part, proj_part, class_part), 'rows')  172 us
    psum x1, blocking collectives, per_device(): pooled = lax.psum(column_sum, 'rows') / total_pixels  111 us
    psum x1, waiting for transfers between devices, per_device(): mixed = lax.psum(mixed_part, 'grp')  68.7 us
    dot_general x3, matrix products, per_device(): jnp.einsum('pd,cd->pc', grad_pre[k + 1], branch_weight[k + 1], preferred_...  68.6 us
    convert_element_type x3, other arithmetic, depth_taps(): outputs.append(total.astype(jnp.bfloat16))  67.9 us
    dynamic_update_slice x2, local copies, waits for them, and re-layouts, ring_gather(): lax.dynamic_update_slice_in_dim(out, from_left, (position - step) % size...  62.9 us
    dynamic_update_slice x1, local copies, waits for them, and re-layouts, ring_gather(): lax.dynamic_update_slice_in_dim(out, from_right, (position + step) % size...  34.9 us
  transfers between devices with their start and end apart: 10, of which 5 were waited for; matrix products, arithmetic and copies ran while one was open for 23% of the time, Pallas kernels for 0%

profile of v1, /device:TPU:0, one launch (start us, length us, event | category | flops | bytes accessed | tf_op | source)
XLA Modules:
  0.0 1022.8 jit_solution(9555941132302764137)
XLA Ops:
  7.2 5.2 fusion.69
  12.4 6.3 collective-permute-start
  20.4 110.5 %psum.49 = f32[512]{0:T(512)S(1)} all-reduce(f32[512]{0:T(512)S(1)} %convert_reduce_fusion), channel_id=1, replica_groups=mesh['rows'=8,'grp'=4] {'rows'}, use_global_device_ids=true, to_apply=%region_2.3 | all-reduce | flops 512 | bytes 4096 | tf_op jit(solution)/shard_map/psum | solution.py:109
  132.2 1.9 convolution_bitcast_fusion.5
  134.2 8.2 maximum_convert_fusion
  142.4 24.1 %add_convert_fusion.1 = bf16[24,128,512]{2,1,0:T(8,128)(2,1)S(1)} fusion(f32[60,128,512]{2,1,0:T(8,128)} %maximum_convert_fusion, f32[512]{0:T(512)S(1)} %bitcast.246, f32[512]{0:T(512)S(1)} %bitcast.247, f32[512]{0:T(512)S(1)} %bitcast.248, f32[512]{0:T(512)S(1)} %bitcast.249, f32[512]{0:T(512)S(1)} %bitcast.250, f32[512]{0:T(512)S(1)} %bitcast.251, ...), kind=kLoop, calls=%fused_computation.49 | loop fusion | flops 28311552 | bytes 37767168 | tf_op jit(solution)/shard_map/convert_element_type | solution.py:58
  166.5 3.8 convolution_bitcast_fusion.3
  170.2 19.2 %add_convert_fusion = bf16[24,128,512]{2,1,0:T(8,128)(2,1)S(1)} fusion(f32[60,128,512]{2,1,0:T(8,128)} %maximum_convert_fusion, f32[512]{0:T(512)S(1)} %bitcast.234, f32[512]{0:T(512)S(1)} %bitcast.235, f32[512]{0:T(512)S(1)} %bitcast.239, f32[512]{0:T(512)S(1)} %bitcast.240, f32[512]{0:T(512)S(1)} %bitcast.241, f32[512]{0:T(512)S(1)} %bitcast.242, ...), kind=kLoop, calls=%fused_computation.48 | loop fusion | flops 28311552 | bytes 37767168 | tf_op jit(solution)/shard_map/convert_element_type | solution.py:58
  189.5 3.8 convolution_bitcast_fusion.2
  193.3 24.6 %add_convert_fusion.2 = bf16[24,128,512]{2,1,0:T(8,128)(2,1)S(1)} fusion(f32[60,128,512]{2,1,0:T(8,128)} %maximum_convert_fusion, f32[512]{0:T(512)S(1)} %bitcast.237, f32[512]{0:T(512)S(1)} %bitcast.238, f32[512]{0:T(512)S(1)} %bitcast.229, f32[512]{0:T(512)S(1)} %bitcast.230, f32[512]{0:T(512)S(1)} %bitcast.231, f32[512]{0:T(512)S(1)} %bitcast.232, ...), kind=kLoop, calls=%fused_computation.50 | loop fusion | flops 28311552 | bytes 37767168 | tf_op jit(solution)/shard_map/convert_element_type | solution.py:58
  219.5 2.7 convolution_bitcast_fusion.4
  222.3 4.8 pad_maximum_fusion
  227.1 15.3 %copy.19 = f32[4,3072,256]{1,0,2:T(4,128)} copy(f32[4,3072,256]{2,1,0:T(8,128)} %pad_maximum_fusion) | data formatting | bytes 25165824 | tf_op jit(solution)/shard_map/stack | solution.py:110
  242.5 12.1 %all-reduce.10.cloned.1.call-start = ((), (), s32[]{:S(2)}) async-start(), calls=%async_computation.1 | async-start | bytes 6291456 | tf_op jit(solution)/shard_map/psum | solution.py:126
  256.9 205.5 %all-reduce.12.cloned.1.call-done = f32[4,3072,256]{1,0,2:T(4,128)} async-done(((f32[4,3072,256]{1,0,2:T(4,128)}), f32[4,3072,256]{1,0,2:T(4,128)}) %all-reduce.12.cloned.1.call-update) | async-done | bytes 12582928
  462.4 2.1 constant_dynamic-slice_fusion
  466.2 3.8 fusion.1
  470.0 68.7 %all-reduce.10.cloned.1.call-done = f32[3072,256]{1,0:T(8,128)} async-done(((f32[3072,256]{1,0:T(8,128)}), f32[3072,256]{1,0:T(8,128)}) %all-reduce.10.cloned.1.call-update) | async-done | bytes 3145744 | tf_op jit(solution)/shard_map/psum | solution.py:126
  538.8 2.6 fusion.73
  541.4 3.2 convert_reduce_fusion.1
  544.6 4.5 fusion.3
  549.1 1.7 collective-permute-start.3
  550.8 34.6 %collective-permute-done.2 = bf16[4,3072,64]{1,2,0:T(8,128)(2,1)} collective-permute-done((bf16[4,3072,64]{1,2,0:T(8,128)(2,1)}, bf16[4,3072,64]{1,2,0:T(8,128)(2,1)}, u32[]{:S(2)}, u32[]{:S(2)}) %collective-permute-start.2) | collective-permute-done | bytes 1572896 | tf_op jit(solution)/shard_map/ppermute | solution.py:20
  585.4 4.1 copy.22
  589.5 3.0 broadcast_in_dim.6
  592.6 30.0 %dynamic_update_slice.12 = bf16[4,3072,256]{2,1,0:T(8,128)(2,1)} dynamic-update-slice(bf16[4,3072,256]{2,1,0:T(8,128)(2,1)} %broadcast_in_dim.6, bf16[4,3072,64]{2,1,0:T(8,128)(2,1)} %copy.22, s32[]{:T(128)} %constant.47.clone.1, s32[]{:T(128)} %constant.47.clone.1, s32[]{:T(128)S(6)} %select_n.27) | dynamic-update-slice | bytes 3145732 | tf_op jit(solution)/shard_map/dynamic_update_slice | solution.py:16
  622.5 2.8 fusion.26
  625.4 5.0 fusion.11
  630.4 4.2 copy.23
  634.5 34.0 %dynamic_update_slice.13 = bf16[4,3072,256]{2,1,0:T(8,128)(2,1)} dynamic-update-slice(bf16[4,3072,256]{2,1,0:T(8,128)(2,1)} %dynamic_update_slice.12, bf16[4,3072,64]{2,1,0:T(8,128)(2,1)} %copy.23, s32[]{:T(128)} %constant.47.clone.1, s32[]{:T(128)} %constant.47.clone.1, s32[]{:T(128)S(6)} %select_n.29) | dynamic-update-slice | bytes 3145732 | tf_op jit(solution)/shard_map/dynamic_update_slice | solution.py:21
  668.5 4.2 copy.24
  672.7 34.9 %dynamic_update_slice.14 = bf16[4,3072,256]{2,1,0:T(8,128)(2,1)} dynamic-update-slice(bf16[4,3072,256]{2,1,0:T(8,128)(2,1)} %dynamic_update_slice.13, bf16[4,3072,64]{2,1,0:T(8,128)(2,1)} %copy.24, s32[]{:T(128)} %constant.47.clone.1, s32[]{:T(128)} %constant.47.clone.1, s32[]{:T(128)S(6)} %select_n.31) | dynamic-update-slice | bytes 3145732 | tf_op jit(solution)/shard_map/dynamic_update_slice | solution.py:26
  707.6 4.2 copy.25
  711.8 28.9 %dynamic_update_slice.15 = bf16[4,3072,256]{2,1,0:T(8,128)(2,1)} dynamic-update-slice(bf16[4,3072,256]{2,1,0:T(8,128)(2,1)} %dynamic_update_slice.14, bf16[4,3072,64]{2,1,0:T(8,128)(2,1)} %copy.25, s32[]{:T(128)} %constant.47.clone.1, s32[]{:T(128)} %constant.47.clone.1, s32[]{:T(128)S(6)} %select_n.33) | dynamic-update-slice | bytes 3145732 | tf_op jit(solution)/shard_map/dynamic_update_slice | solution.py:21
  740.7 4.5 fusion.68
  745.9 3.8 fusion.14
  749.8 1.8 fusion.17
  751.6 1.8 fusion.20
  753.3 1.8 fusion.23
  755.1 24.8 %multiply_reduce_fusion.18 = (f32[512]{0:T(512)S(1)}, f32[512]{0:T(512)S(1)}, f32[512]{0:T(512)S(1)}, f32[512]{0:T(512)S(1)}, f32[512]{0:T(512)S(1)}, /*index=5*...) fusion(f32[60,128,512]{2,1,0:T(8,128)} %maximum_convert_fusion, ...), kind=kOutput, calls=%fused_computation.38 | convolution fusion | flops 833613312 | bytes 36456448 | tf_op jit(solution)/shard_map/pd,cd->pc/dot_general | solution.py:147
  780.0 24.3 %multiply_reduce_fusion.9 = (f32[512]{0:T(512)S(1)}, f32[512]{0:T(512)S(1)}, f32[512]{0:T(512)S(1)}, f32[512]{0:T(512)S(1)}, f32[512]{0:T(512)S(1)}, /*index=5*/...) fusion(f32[60,128,512]{2,1,0:T(8,128)} %maximum_convert_fusion, ...), kind=kOutput, calls=%fused_computation.29 | convolution fusion | flops 833613312 | bytes 36456448 | tf_op jit(solution)/shard_map/pd,cd->pc/dot_general | solution.py:147
  804.4 19.6 %multiply_reduce_fusion = (f32[512]{0:T(512)S(1)}, f32[512]{0:T(512)S(1)}, f32[512]{0:T(512)S(1)}, f32[512]{0:T(512)S(1)}, f32[512]{0:T(512)S(1)}, /*index=5*/f3...) fusion(f32[60,128,512]{2,1,0:T(8,128)} %maximum_convert_fusion, ...), kind=kOutput, calls=%fused_computation.20 | convolution fusion | flops 833613312 | bytes 36456448 | tf_op jit(solution)/shard_map/pd,cd->pc/dot_general | solution.py:147
  824.8 2.5 pad_maximum_fusion.1
  828.0 67.9 %all-reduce.14.cloned.1.call-done = (f32[3,3,3,512]{3,2,1,0:T(4,128)}, f32[256]{0:T(256)}, f32[256,11]{0,1:T(8,128)}) async-done(((f32[3,3,3,512]{3,2,1,0:T(4,128)}, f32[256]{0:T(256)}, f32[256,11]{0,1:T(8,128)}), (f32[3,3,3,512]{3,2,1,0:T(4,128)}, f32[256]{0:T(256)}, f32[256,11]{0,1:T(8,128)})) %all-reduce.14.cloned.1.call-update) | async-done | bytes 67600 | tf_op jit(solution)/shard_map/psum | solution.py:154
  897.1 5.6 all-reduce.1
  904.4 104.3 %all-reduce.16.cloned.1.call-done = (f32[4,512,256]{1,2,0:T(8,128)}, f32[4,64,256]{2,1,0:T(8,128)}) async-done(((f32[4,512,256]{1,2,0:T(8,128)}, f32[4,64,256]{2,1,0:T(8,128)}), (f32[4,512,256]{1,2,0:T(8,128)}, f32[4,64,256]{2,1,0:T(8,128)})) %all-reduce.16.cloned.1.call-update) | async-done | bytes 2359312 | tf_op jit(solution)/shard_map/psum | solution.py:154
  1008.6 2.9 copy.33
  1011.5 1.7 pad_maximum_fusion.2
  (90 shorter events, 15.3 us)
Async XLA Ops:
  7.2 123.8 %copy-start = (bf16[512,256]{1,0:T(8,128)(2,1)S(1)}, bf16[512,256]{1,0:T(8,128)(2,1)}, u32[]{:S(2)}) copy-start(bf16[512,256]{1,0:T(8,128)(2,1)} %param.10) | copy-start | bytes 786436
  7.2 12.8 %copy-start.2 = (bf16[24,128,512]{2,1,0:T(8,128)(2,1)S(1)}, bf16[24,128,512]{2,1,0:T(8,128)(2,1)}, u32[]{:S(2)}) copy-start(bf16[24,128,512]{2,1,0:T(8,128)(2,1)} %param.7) | copy-start | bytes 9437188
  7.2 125.0 %copy-start.20 = (f32[3,3,3,512]{3,2,1,0:T(4,128)S(1)}, f32[3,3,3,512]{3,2,1,0:T(4,128)}, u32[]{:S(2)}) copy-start(f32[3,3,3,512]{3,2,1,0:T(4,128)} %param.8) | copy-start | bytes 165892
  7.2 248.7 %reduce-scatter.4.cloned.1.call-start = ((), (), s32[]{:S(2)}) async-start(), calls=%async_computation.2 | async-start | bytes 163840
  12.4 121.8 %collective-permute-start = (bf16[18,128,512]{2,1,0:T(8,128)(2,1)}, bf16[18,128,512]{2,1,0:T(8,128)(2,1)}, u32[]{:S(2)}, u32[]{:S(2)}) collective-permute-start(bf16[18,128,512]{2,1,0:T(8,128)(2,1)} %get-tuple-element.50), channel_id=1, source_target_pairs={{0,4},{4,8},{8,12},{12,16},{16,20},{20,24},{24,28},{1,5},{5,9},{9,... | collective-permute-start | bytes 7077896 | tf_op jit(solution)/shard_map/ppermute | solution.py:37
  18.7 115.5 %collective-permute-start.1 = (bf16[18,128,512]{2,1,0:T(8,128)(2,1)}, bf16[18,128,512]{2,1,0:T(8,128)(2,1)}, u32[]{:S(2)}, u32[]{:S(2)}) collective-permute-start(bf16[18,128,512]{2,1,0:T(8,128)(2,1)} %get-tuple-element.51), channel_id=1, source_target_pairs={{4,0},{8,4},{12,8},{16,12},{20,16},{24,20},{28,24},{5,1},{9,5},{13... | collective-permute-start | bytes 7077896 | tf_op jit(solution)/shard_map/ppermute | solution.py:40
  132.1 330.3 %all-reduce.12.cloned.1.call-start = ((), (), s32[]{:S(2)}) async-start(), calls=%async_computation.3 | async-start | bytes 25165824
  166.4 23.0 %copy-start.4 = (bf16[24,128,512]{2,1,0:T(8,128)(2,1)}, bf16[24,128,512]{2,1,0:T(8,128)(2,1)S(1)}, u32[]{:S(2)}) copy-start(bf16[24,128,512]{2,1,0:T(8,128)(2,1)S(1)} %add_convert_fusion.1) | copy-start | bytes 9437188
  189.5 28.4 %copy-start.6 = (bf16[24,128,512]{2,1,0:T(8,128)(2,1)}, bf16[24,128,512]{2,1,0:T(8,128)(2,1)S(1)}, u32[]{:S(2)}) copy-start(bf16[24,128,512]{2,1,0:T(8,128)(2,1)S(1)} %add_convert_fusion) | copy-start | bytes 9437188
  217.9 1.6 copy-start.8
  217.9 4.3 copy-start.9
  217.9 4.3 copy-start.10
  242.4 12.1 %copy-start.23 = (u32[32]{0:T(128)S(1)}, u32[32]{0:T(128)}, u32[]{:S(2)}) copy-start(u32[32]{0:T(128)} %constant.60) | copy-start | bytes 388
  242.4 14.3 %copy-start.22 = (bf16[5,64,256]{2,1,0:T(8,128)(2,1)S(1)}, bf16[5,64,256]{2,1,0:T(8,128)(2,1)}, u32[]{:S(2)}) copy-start(bf16[5,64,256]{2,1,0:T(8,128)(2,1)} %param.11) | copy-start | bytes 491524
  242.5 296.3 %all-reduce.10.cloned.1.call-start = ((), (), s32[]{:S(2)}) async-start(), calls=%async_computation.1 | async-start | bytes 6291456 | tf_op jit(solution)/shard_map/psum | solution.py:126
  464.5 1.7 copy-start.11
  464.5 5.5 copy-start.19
  464.5 74.3 %copy-start.21 = (bf16[256,11]{0,1:T(8,128)(2,1)S(1)}, bf16[256,11]{0,1:T(8,128)(2,1)}, u32[]{:S(2)}) copy-start(bf16[256,11]{0,1:T(8,128)(2,1)} %param.12) | copy-start | bytes 16900
  470.0 426.0 %all-reduce.14.cloned.1.call-start = ((), (), s32[]{:S(2)}) async-start(), calls=%async_computation.4 | async-start | bytes 182272 | tf_op jit(solution)/shard_map/psum | solution.py:154
  538.8 5.8 copy-start.12
  544.6 4.5 copy-start.15
  549.1 36.3 %collective-permute-start.2 = (bf16[4,3072,64]{1,2,0:T(8,128)(2,1)}, bf16[4,3072,64]{1,2,0:T(8,128)(2,1)}, u32[]{:S(2)}, u32[]{:S(2)}) collective-permute-start(bf16[4,3072,64]{1,2,0:T(8,128)(2,1)} %fusion.3), channel_id=1, source_target_pairs={{0,1},{1,2},{2,3},{3,0},{4,5},{5,6},{6,7},{7,4},{8,9},{9,10},{10,1... | collective-permute-start | bytes 4718600 | tf_op jit(solution)/shard_map/ppermute | solution.py:20
  549.1 119.5 %collective-permute-start.3 = (bf16[4,3072,64]{1,2,0:T(8,128)(2,1)}, bf16[4,3072,64]{1,2,0:T(8,128)(2,1)}, u32[]{:S(2)}, u32[]{:S(2)}) collective-permute-start(bf16[4,3072,64]{1,2,0:T(8,128)(2,1)} %fusion.3), channel_id=1, source_target_pairs={{0,3},{1,0},{2,1},{3,2},{4,7},{5,4},{6,5},{7,6},{8,11},{9,8},{10,9... | collective-permute-start | bytes 4718600 | tf_op jit(solution)/shard_map/ppermute | solution.py:25
  585.4 122.2 %collective-permute-start.4 = (bf16[4,3072,64]{1,2,0:T(8,128)(2,1)}, bf16[4,3072,64]{1,2,0:T(8,128)(2,1)}, u32[]{:S(2)}, u32[]{:S(2)}) collective-permute-start(bf16[4,3072,64]{1,2,0:T(8,128)(2,1)} %collective-permute-done.2), channel_id=1, source_target_pairs={{0,1},{1,2},{2,3},{3,0},{4,5},{5,6},{6,7},{7,4},{8,9},{9,10},{10,1... | collective-permute-start | bytes 4718600 | tf_op jit(solution)/shard_map/ppermute | solution.py:20
  740.7 5.2 copy-start.3
  740.7 9.0 copy-start.5
  745.9 5.6 copy-start.7
  755.1 24.9 %copy-start.14 = (bf16[1,3072,256]{2,1,0:T(8,128)(2,1)S(1)}, bf16[1,3072,256]{2,1,0:T(8,128)(2,1)}, u32[]{:S(2)}) copy-start(bf16[1,3072,256]{2,1,0:T(8,128)(2,1)} %get-tuple-element.49) | copy-start | bytes 4718596
  780.0 24.4 %copy-start.13 = (bf16[1,3072,256]{2,1,0:T(8,128)(2,1)S(1)}, bf16[1,3072,256]{2,1,0:T(8,128)(2,1)}, u32[]{:S(2)}) copy-start(bf16[1,3072,256]{2,1,0:T(8,128)(2,1)} %get-tuple-element.48) | copy-start | bytes 4718596
  804.4 20.4 %copy-start.16 = (f32[1,512,256]{1,2,0:T(8,128)S(1)}, f32[1,512,256]{1,2,0:T(8,128)}, u32[]{:S(2)}) copy-start(f32[1,512,256]{1,2,0:T(8,128)} %fusion.14) | copy-start | bytes 1572868
  804.4 20.4 %copy-start.17 = (f32[1,512,256]{1,2,0:T(8,128)S(1)}, f32[1,512,256]{1,2,0:T(8,128)}, u32[]{:S(2)}) copy-start(f32[1,512,256]{1,2,0:T(8,128)} %fusion.17) | copy-start | bytes 1572868
  804.4 20.4 %copy-start.18 = (f32[1,512,256]{1,2,0:T(8,128)S(1)}, f32[1,512,256]{1,2,0:T(8,128)}, u32[]{:S(2)}) copy-start(f32[1,512,256]{1,2,0:T(8,128)} %fusion.20) | copy-start | bytes 1572868
  824.0 192.1 %copy-start.1 = (bf16[512,256]{1,0:T(8,128)(2,1)S(1)}, bf16[512,256]{1,0:T(8,128)(2,1)}, u32[]{:S(2)}) copy-start(bf16[512,256]{1,0:T(8,128)(2,1)} %param.10) | copy-start | bytes 786436
  824.7 183.9 %all-reduce.16.cloned.1.call-start = ((), (), s32[]{:S(2)}) async-start(), calls=%async_computation.5 | async-start | bytes 4718592 | tf_op jit(solution)/shard_map/psum | solution.py:154
Sparse Core Ops, SparseCore 0:
  132.2 18.7 reduce-scatter.3
  242.6 219.7 all-reduce.11
  470.1 68.6 all-reduce.9
  824.9 71.0 all-reduce.13
  900.4 108.2 all-reduce.15
